TPU v7x, 256 devices: a whole 4x4x8 slice. The times are simulated.
256 devices in a mesh: lat: 16 (over z, x_lo), lon: 16 (over y, x_hi, core).
Axes of the slice: x: 4 (x_hi: 2, x_lo: 2; x = x_hi * 2 + x_lo), y: 4, z: 8, core: 2. Of those that a mesh axis runs over, the one named last changes fastest.
Arguments:
- fine_tokens: bfloat16 [192, 384, 512], P('lat', 'lon'), may hold values from -6 to 6
- region_labels: int32 [192, 384], P('lat', 'lon'), may hold values from 0 to 5, as said below
- fine_attention_gain: float32 [512], replicated, may hold values from 0.5 to 1.5
- fine_triple_weight: bfloat16 [512, 1536], replicated, may hold values from -0.25 to 0.25
- fine_output_weight: bfloat16 [512, 512], replicated, may hold values from -0.25 to 0.25
- fine_hidden_gain: float32 [512], replicated, may hold values from 0.5 to 1.5
- fine_up_weight: bfloat16 [512, 2048], replicated, may hold values from -0.25 to 0.25
- fine_down_weight: bfloat16 [2048, 512], replicated, may hold values from -0.125 to 0.125
- merge_gain: float32 [2048], replicated, may hold values from 0.5 to 1.5
- merge_weight: bfloat16 [2048, 1024], P('lon'), may hold values from -0.125 to 0.125
- coarse_attention_gain: float32 [1024], replicated, may hold values from 0.5 to 1.5
- coarse_triple_weight: bfloat16 [1024, 3072], P(None, 'lon'), may hold values from -0.1875 to 0.1875
- coarse_output_weight: bfloat16 [1024, 1024], P('lon'), may hold values from -0.1875 to 0.1875
- coarse_hidden_gain: float32 [1024], replicated, may hold values from 0.5 to 1.5
- coarse_up_weight: bfloat16 [1024, 4096], P(None, 'lon'), may hold values from -0.1875 to 0.1875
- coarse_down_weight: bfloat16 [4096, 1024], P('lon'), may hold values from -0.09375 to 0.09375
- skip_cotangent: bfloat16 [192, 384, 512], P('lat', 'lon'), may hold values from -6 to 6
- coarse_cotangent: bfloat16 [96, 192, 1024], P('lat', 'lon'), may hold values from -6 to 6
Outputs:
- skip_tokens: bfloat16 [192, 384, 512], P('lat', 'lon')
- coarse_tokens: bfloat16 [96, 192, 1024], P('lat', 'lon')
- token_gradient: bfloat16 [192, 384, 512], P('lat', 'lon')
Inputs may be any that keep to these rules, and one draw needn't show every extreme that they name: `region_labels`: tokens attend only within their window to tokens of the same label. The last 3 rows of the shifted grid carry label 1, all other rows label 0.
All inputs are finite; a program needn't handle non-finite values.
Results may differ from a plain program's by a relative error of at most 0.025.
Values may be sent and summed in bfloat16 or wider, within the bound.
A program may use at most 128 MiB of HBM per device.

v0:
```python
import jax
import jax.numpy as jnp
from jax import lax
from jax.sharding import PartitionSpec as P

HEADS1 = 8
HEADS2 = 16
WIN_LAT = 6
WIN_LON = 12


EPSILON = 1e-05


def from_behind(block, axis, distance):
    devices = range(lax.axis_size(axis))
    route = [((i - distance) % len(devices), i) for i in devices]
    return lax.ppermute(block, axis, route)


def layer_norm(norm_input, gain_vector):
    average = jnp.mean(norm_input, axis=-1, keepdims=True)
    centred = norm_input - average
    variance = jnp.mean(centred * centred, axis=-1, keepdims=True)
    return centred * lax.rsqrt(variance + EPSILON) * gain_vector


def to_windows(tile_field, win_rows, win_cols):
    row_count = tile_field.shape[0]
    col_count = tile_field.shape[1]
    feat_count = tile_field.shape[2]
    blocks = tile_field.reshape(
        row_count // win_rows, win_rows, col_count // win_cols, win_cols, feat_count
    )
    blocks = blocks.transpose(0, 2, 1, 3, 4)
    return blocks.reshape(
        row_count // win_rows * (col_count // win_cols), win_rows * win_cols, feat_count
    )


def from_windows(blocks, row_count, col_count, win_rows, win_cols):
    feat_count = blocks.shape[-1]
    tile_field = blocks.reshape(
        row_count // win_rows, col_count // win_cols, win_rows, win_cols, feat_count
    )
    return tile_field.transpose(0, 2, 1, 3, 4).reshape(row_count, col_count, feat_count)


def window_attention(normed, triple_weight, output_weight, labels, head_count):
    row_count, col_count, feat_width = normed.shape
    head_size = triple_weight.shape[1] // (3 * head_count)
    packed = jnp.dot(
        normed.reshape(row_count * col_count, feat_width),
        triple_weight,
        preferred_element_type=jnp.float32,
    ).astype(jnp.bfloat16)
    packed = to_windows(
        packed.reshape(row_count, col_count, 3 * head_count * head_size), WIN_LAT, WIN_LON
    )
    window_count = packed.shape[0]
    window_size = WIN_LAT * WIN_LON
    packed = packed.reshape(window_count, window_size, head_count, 3, head_size)
    queries = packed[:, :, :, 0]
    key_part = packed[:, :, :, 1]
    value_part = packed[:, :, :, 2]
    scores = jnp.einsum(
        "wqhd,wkhd->whqk", queries, key_part, preferred_element_type=jnp.float32
    ) * head_size ** (-0.5)
    weights = jnp.exp(scores)
    if labels is not None:
        label_blocks = to_windows(
            labels.reshape(row_count, col_count, 1), WIN_LAT, WIN_LON
        ).reshape(window_count, window_size)
        same_region = (label_blocks[:, :, None] == label_blocks[:, None, :]).astype(jnp.float32)
        weights = weights * same_region[:, None]
    attn_probs = (weights / jnp.sum(weights, axis=-1, keepdims=True)).astype(jnp.bfloat16)
    mixed_heads = jnp.einsum(
        "whqk,wkhd->wqhd", attn_probs, value_part, preferred_element_type=jnp.float32
    ).astype(jnp.bfloat16)
    mixed_heads = from_windows(
        mixed_heads.reshape(window_count, window_size, head_count * head_size),
        row_count,
        col_count,
        WIN_LAT,
        WIN_LON,
    )
    projected = jnp.dot(
        mixed_heads.reshape(row_count * col_count, head_count * head_size),
        output_weight,
        preferred_element_type=jnp.float32,
    )
    return projected.reshape(row_count, col_count, output_weight.shape[1])


def hidden_part(normed, up_weight, down_weight):
    feat_width = normed.shape[-1]
    lifted = jnp.dot(normed.reshape(-1, feat_width), up_weight, preferred_element_type=jnp.float32)
    active = jax.nn.gelu(lifted, approximate=False).astype(jnp.bfloat16)
    lowered = jnp.dot(active, down_weight, preferred_element_type=jnp.float32)
    return lowered.reshape(normed.shape[:-1] + (down_weight.shape[1],))


def fine_block(
    fine_start,
    labels,
    attention_gain,
    triple_weight,
    output_weight,
    hidden_gain,
    up_weight,
    down_weight,
):
    normed = layer_norm(fine_start, attention_gain).astype(jnp.bfloat16)
    residual = fine_start + window_attention(normed, triple_weight, output_weight, labels, HEADS1)
    normed_two = layer_norm(residual, hidden_gain).astype(jnp.bfloat16)
    return (residual + hidden_part(normed_two, up_weight, down_weight)).astype(jnp.bfloat16)


def merge_patches(skip_float, merge_gain, merge_weight):
    row_count, col_count, feat_width = skip_float.shape
    quad_blocks = skip_float.reshape(row_count // 2, 2, col_count // 2, 2, feat_width).transpose(
        0, 2, 3, 1, 4
    )
    joined = quad_blocks.reshape(row_count // 2, col_count // 2, 4 * feat_width)
    normed = layer_norm(joined, merge_gain).astype(jnp.bfloat16)
    projected = jnp.dot(
        normed.reshape(-1, 4 * feat_width), merge_weight, preferred_element_type=jnp.float32
    )
    return projected.astype(jnp.bfloat16).reshape(
        row_count // 2, col_count // 2, merge_weight.shape[1]
    )


def roll_forward(tile_field, lat_step, lon_step):
    south_rim = from_behind(tile_field[:lat_step], "lat", -1)
    taller = jnp.concatenate([tile_field[lat_step:], south_rim], axis=0)
    beside = from_behind(taller[:, :lon_step], "lon", -1)
    return jnp.concatenate([taller[:, lon_step:], beside], axis=1)


def roll_back(tile_field, lat_step, lon_step):
    north_rim = from_behind(tile_field[-lat_step:], "lat", 1)
    taller = jnp.concatenate([north_rim, tile_field[:-lat_step]], axis=0)
    beside = from_behind(taller[:, -lon_step:], "lon", 1)
    return jnp.concatenate([beside, taller[:, :-lon_step]], axis=1)


def local(
    fine_tokens,
    region_labels,
    fine_attention_gain,
    fine_triple_weight,
    fine_output_weight,
    fine_hidden_gain,
    fine_up_weight,
    fine_down_weight,
    merge_gain,
    merge_weight,
    coarse_attention_gain,
    coarse_triple_weight,
    coarse_output_weight,
    coarse_hidden_gain,
    coarse_up_weight,
    coarse_down_weight,
    skip_cotangent,
    coarse_cotangent,
):
    lat_step = WIN_LAT // 2
    lon_step = WIN_LON // 2
    rolled = roll_forward(fine_tokens, lat_step, lon_step)

    def fine_map(fine_start):
        return fine_block(
            fine_start,
            region_labels,
            fine_attention_gain,
            fine_triple_weight,
            fine_output_weight,
            fine_hidden_gain,
            fine_up_weight,
            fine_down_weight,
        )

    rolled_out, fine_pull = jax.vjp(fine_map, rolled.astype(jnp.float32))
    skip_tokens = roll_back(rolled_out, lat_step, lon_step)
    full_merge = lax.all_gather(merge_weight, "lon", axis=0, tiled=True)

    def merge_map(skip_float):
        return merge_patches(skip_float, merge_gain, full_merge)

    merged, merge_pull = jax.vjp(merge_map, skip_tokens.astype(jnp.float32))
    coarse_input = merged.astype(jnp.float32)

    def first_norm(norm_input):
        return layer_norm(norm_input, coarse_attention_gain)

    def second_norm(norm_input):
        return layer_norm(norm_input, coarse_hidden_gain)

    normed_first, first_pull = jax.vjp(first_norm, coarse_input)
    normed_one = normed_first.astype(jnp.bfloat16)
    group_count = lax.axis_size("lon")
    group_heads = HEADS2 // group_count
    cotangent_float = coarse_cotangent.astype(jnp.float32)

    def local_attention(norm_value):
        return window_attention(
            norm_value, coarse_triple_weight, coarse_output_weight, None, group_heads
        )

    def local_hidden(norm_value):
        return hidden_part(norm_value, coarse_up_weight, coarse_down_weight)

    band_one = lax.all_gather(normed_one, "lon", axis=1, tiled=True)
    attention_term, attention_pull = jax.vjp(local_attention, band_one)
    coarse_attended = lax.psum_scatter(
        attention_term.astype(jnp.bfloat16), "lon", scatter_dimension=1, tiled=True
    ).astype(jnp.float32)
    coarse_residual = coarse_input + coarse_attended
    normed_second, second_pull = jax.vjp(second_norm, coarse_residual)
    band_two = lax.all_gather(normed_second.astype(jnp.bfloat16), "lon", axis=1, tiled=True)
    hidden_term, hidden_pull = jax.vjp(local_hidden, band_two)
    coarse_hidden = lax.psum_scatter(
        hidden_term.astype(jnp.bfloat16), "lon", scatter_dimension=1, tiled=True
    ).astype(jnp.float32)
    coarse_tokens = (coarse_residual + coarse_hidden).astype(jnp.bfloat16)
    cotangent_band = lax.all_gather(coarse_cotangent, "lon", axis=1, tiled=True)
    hidden_grad = hidden_pull(cotangent_band.astype(jnp.float32))[0]
    grad_two = lax.psum_scatter(
        hidden_grad.astype(jnp.float32).astype(jnp.bfloat16), "lon", scatter_dimension=1, tiled=True
    ).astype(jnp.float32)
    grad_residual = cotangent_float + second_pull(grad_two)[0]
    grad_band = lax.all_gather(grad_residual.astype(jnp.bfloat16), "lon", axis=1, tiled=True)
    attention_grad = attention_pull(grad_band.astype(jnp.float32))[0]
    grad_one = lax.psum_scatter(
        attention_grad.astype(jnp.float32).astype(jnp.bfloat16),
        "lon",
        scatter_dimension=1,
        tiled=True,
    ).astype(jnp.float32)
    grad_merged = grad_residual + first_pull(grad_one)[0]
    grad_from_merge = merge_pull(grad_merged.astype(jnp.bfloat16))[0]
    grad_skip = (skip_cotangent.astype(jnp.float32) + grad_from_merge).astype(jnp.bfloat16)
    grad_rolled = roll_forward(grad_skip, lat_step, lon_step)
    grad_start = fine_pull(grad_rolled)[0]
    token_gradient = roll_back(grad_start.astype(jnp.bfloat16), lat_step, lon_step)
    return (skip_tokens, coarse_tokens, token_gradient)


def solution(mesh):
    in_specs = (
        P("lat", "lon", None),
        P("lat", "lon"),
        P(),
        P(),
        P(),
        P(),
        P(),
        P(),
        P(),
        P("lon", None),
        P(),
        P(None, "lon"),
        P("lon", None),
        P(),
        P(None, "lon"),
        P("lon", None),
        P("lat", "lon", None),
        P("lat", "lon", None),
    )
    out_specs = (P("lat", "lon", None), P("lat", "lon", None), P("lat", "lon", None))
    return jax.shard_map(local, mesh=mesh, in_specs=in_specs, out_specs=out_specs, check_vma=False)
```

profile of v0, /device:TPU:8, one launch (start us, length us, event | category | flops | bytes accessed | tf_op | source)
XLA Modules:
  0.0 984.7 jit_solution(8161141125917931714)
XLA Ops:
  8.9 6.8 collective-permute-start
  31.1 5.8 reshape.418
  36.9 8.2 fusion.118
  45.1 3.6 copy.328
  51.3 3.8 copy.327
  65.8 6.3 fusion.10
  74.6 7.0 collective-permute-done.2
  82.1 6.3 collective-permute-done.3
  95.7 4.1 fusion.121
  105.7 51.7 %all-gather.8.cloned.1.call-done = bf16[6,192,1024]{2,0,1:T(8,128)(2,1)} async-done(((bf16[6,12,1024]{2,0,1:T(8,128)(2,1)}), bf16[6,192,1024]{2,0,1:T(8,128)(2,1)}) %all-gather.8.cloned.1.call-update) | async-done | bytes 2359312 | tf_op jit(solution)/shard_map/all_gather | solution.py:214
  168.8 3.4 reshape.426
  172.2 5.0 fusion.119
  198.9 141.2 %all-reduce.15.cloned.1.call-done = bf16[6,192,1024]{2,1,0:T(8,128)(2,1)} async-done(((bf16[6,192,1024]{2,1,0:T(8,128)(2,1)}), bf16[6,192,1024]{2,1,0:T(8,128)(2,1)}) %all-reduce.15.cloned.1.call-update) | async-done | bytes 2359312
  346.6 59.8 %all-gather.12.cloned.1.call-done = bf16[6,192,1024]{2,0,1:T(8,128)(2,1)} async-done(((bf16[6,12,1024]{2,0,1:T(8,128)(2,1)}), bf16[6,192,1024]{2,0,1:T(8,128)(2,1)}) %all-gather.12.cloned.1.call-update) | async-done | bytes 2359312 | tf_op jit(solution)/shard_map/all_gather | solution.py:227
  406.5 4.7 copy.277
  411.2 53.2 %all-gather.10.cloned.1.call-done = bf16[6,192,1024]{2,0,1:T(8,128)(2,1)} async-done(((bf16[6,12,1024]{2,0,1:T(8,128)(2,1)}), bf16[6,192,1024]{2,0,1:T(8,128)(2,1)}) %all-gather.10.cloned.1.call-update) | async-done | bytes 2359312 | tf_op jit(solution)/shard_map/all_gather | solution.py:221
  464.3 3.2 copy.273
  469.4 8.6 convolution_convert_fusion
  478.1 144.6 %all-reduce.17.cloned.1.call-done = bf16[6,192,1024]{2,1,0:T(8,128)(2,1)} async-done(((bf16[6,192,1024]{2,1,0:T(8,128)(2,1)}), bf16[6,192,1024]{2,1,0:T(8,128)(2,1)}) %all-reduce.17.cloned.1.call-update) | async-done | bytes 2359312
  628.9 5.9 convolution_convert_fusion.2
  634.8 57.1 %all-gather.14.cloned.1.call-done = bf16[6,192,1024]{2,0,1:T(8,128)(2,1)} async-done(((bf16[6,12,1024]{2,0,1:T(8,128)(2,1)}), bf16[6,192,1024]{2,0,1:T(8,128)(2,1)}) %all-gather.14.cloned.1.call-update) | async-done | bytes 2359312 | tf_op jit(solution)/shard_map/all_gather | solution.py:233
  708.8 3.6 copy.291
  712.4 3.3 reshape.438
  720.1 3.4 convolution_convert_fusion.1
  725.5 155.0 %all-reduce.19.cloned.1.call-done = (bf16[6,192,1024]{2,1,0:T(8,128)(2,1)}, bf16[6,192,1024]{2,1,0:T(8,128)(2,1)}) async-done(((bf16[6,192,1024]{2,1,0:T(8,128)(2,1)}, bf16[6,192,1024]{2,1,0:T(8,128)(2,1)}), (bf16[6,192,1024]{2,1,0:T(8,128)(2,1)}, bf16[6,192,1024]{2,1,0:T(8,128)(2,1)})) %all-reduce.19.cloned.1.call-update) | async-done | bytes 4718608
  898.6 4.5 fusion.16
  914.1 3.4 collective-permute-start.4
  924.0 4.8 fusion.27
  943.4 5.4 copy.307
  948.8 4.7 reshape.447
  963.6 6.4 collective-permute-done.6
  970.9 5.7 collective-permute-done.7
  (354 shorter events, 177.5 us)
Async XLA Ops:
  7.2 58.6 %copy-start = (bf16[512,2048]{1,0:T(8,128)(2,1)S(1)}, bf16[512,2048]{1,0:T(8,128)(2,1)}, u32[]{:S(2)}) copy-start(bf16[512,2048]{1,0:T(8,128)(2,1)} %param.24) | copy-start | bytes 6291460
  7.2 88.5 %all-gather.6.cloned.1.call-start = ((), (), s32[]{:S(2)}) async-start(), calls=%async_computation | async-start | bytes 4456448 | tf_op jit(solution)/shard_map/all_gather | solution.py:186
  7.9 149.4 %all-gather.8.cloned.1.call-start = ((), (), s32[]{:S(2)}) async-start(), calls=%async_computation.1 | async-start | bytes 3342336 | tf_op jit(solution)/shard_map/all_gather | solution.py:214
  8.9 8.8 collective-permute-start
  16.6 40.2 %copy-start.27 = (f32[4,72,72]{1,2,0:T(8,128)}, f32[4,72,72]{1,2,0:T(8,128)S(1)}, u32[]{:S(2)}) copy-start(f32[4,72,72]{1,2,0:T(8,128)S(1)} %compare_convert_fusion) | copy-start | bytes 248836
  17.7 4.1 collective-permute-start.1
  19.6 44.2 %copy-start.1 = (bf16[12,18,512]{2,1,0:T(8,128)(2,1)}, bf16[12,18,512]{2,1,0:T(8,128)(2,1)S(1)}, u32[]{:S(2)}) copy-start(bf16[12,18,512]{2,1,0:T(8,128)(2,1)S(1)} %slice_maximum_fusion.1) | copy-start | bytes 663556
  21.7 42.1 %copy-start.14 = (bf16[12,6,512]{2,1,0:T(8,128)(2,1)}, bf16[12,6,512]{2,1,0:T(8,128)(2,1)S(1)}, u32[]{:S(2)}) copy-start(bf16[12,6,512]{2,1,0:T(8,128)(2,1)S(1)} %collective-permute-done.1) | copy-start | bytes 221188
  51.3 5.5 copy-start.19
  65.6 6.6 copy-start.49
  65.6 6.5 copy-start.38
  65.8 6.4 copy-start.25
  74.5 7.1 collective-permute-start.2
  81.7 6.7 collective-permute-start.3
  95.7 8.0 copy-start.53
  103.6 57.0 %copy-start.40 = (f32[6,12]{0,1:T(8,128)}, f32[6,12]{0,1:T(8,128)S(1)}, u32[]{:S(2)}) copy-start(f32[6,12]{0,1:T(8,128)S(1)} %copy.256) | copy-start | bytes 868
  105.6 234.5 %all-reduce.15.cloned.1.call-start = ((), (), s32[]{:S(2)}) async-start(), calls=%async_computation.5 | async-start | bytes 4718592
  186.7 5.6 copy-start.35
  195.5 149.2 %copy-start.44 = (f32[1024]{0:T(1024)S(1)}, f32[1024]{0:T(1024)}, u32[]{:S(2)}) copy-start(f32[1024]{0:T(1024)} %param.31) | copy-start | bytes 12292
  195.5 210.9 %all-gather.12.cloned.1.call-start = ((), (), s32[]{:S(2)}) async-start(), calls=%async_computation.3 | async-start | bytes 3342336 | tf_op jit(solution)/shard_map/all_gather | solution.py:227
  197.2 267.1 %all-gather.10.cloned.1.call-start = ((), (), s32[]{:S(2)}) async-start(), calls=%async_computation.2 | async-start | bytes 3342336 | tf_op jit(solution)/shard_map/all_gather | solution.py:221
  346.6 276.0 %all-reduce.17.cloned.1.call-start = ((), (), s32[]{:S(2)}) async-start(), calls=%async_computation.6 | async-start | bytes 4718592
  478.0 213.9 %all-gather.14.cloned.1.call-start = ((), (), s32[]{:S(2)}) async-start(), calls=%async_computation.4 | async-start | bytes 3342336 | tf_op jit(solution)/shard_map/all_gather | solution.py:233
  628.6 251.9 %all-reduce.19.cloned.1.call-start = ((), (), s32[]{:S(2)}) async-start(), calls=%async_computation.7 | async-start | bytes 9437184
  723.5 159.6 %copy-start.54 = (f32[1024]{0:T(1024)S(1)}, f32[1024]{0:T(1024)}, u32[]{:S(2)}) copy-start(f32[1024]{0:T(1024)} %param.28) | copy-start | bytes 12292
  724.2 164.9 %copy-start.41 = (f32[6,12]{0,1:T(8,128)S(1)}, f32[6,12]{0,1:T(8,128)}, u32[]{:S(2)}) copy-start(f32[6,12]{0,1:T(8,128)} %copy-done.40) | copy-start | bytes 868
  911.6 6.0 copy-start.56
  914.1 5.4 collective-permute-start.4
  919.5 4.5 collective-permute-start.5
  961.9 8.3 copy-start.34
  963.5 6.5 collective-permute-start.6
  970.0 6.5 collective-permute-start.7
  (62 other events, 161.3 us)
Sparse Core Ops, SparseCore 0:
  10.8 61.9 all-gather.5
  105.7 51.5 all-gather.7
  195.7 144.4 all-reduce.14
  343.3 63.1 all-gather.11
  409.6 54.6 all-gather.9
  478.1 144.4 all-reduce.16
  628.7 63.0 all-gather.13
  723.6 156.8 all-reduce.18
where the time goes:
time: 1000 us; the launch traced here: 985 us
  waiting for transfers between devices  695 us (70%)
  local copies, waits for them, and re-layouts  150 us (15%)
  matrix products  67.6 us (7%)
  other arithmetic  40 us (4%)
  between operations  16.4 us (2%)
  starting transfers between devices  15.8 us (2%)
    unnamed x11, waiting for transfers between devices  442 us
    all_gather x1, waiting for transfers between devices, local(): cotangent_band = lax.all_gather(coarse_cotangent, 'lon', axis=1, tiled=True)  59.8 us
    all_gather x1, waiting for transfers between devices, local(): lax.all_gather(grad_residual.astype(jnp.bfloat16), 'lon', axis=1, tiled=T...  57.1 us
    all_gather x1, waiting for transfers between devices, local(): lax.all_gather(normed_second.astype(jnp.bfloat16), 'lon', axis=1, tiled=T...  53.2 us
    all_gather x1, waiting for transfers between devices, local(): band_one = lax.all_gather(normed_one, 'lon', axis=1, tiled=True)  51.7 us
    ppermute x8, waiting for transfers between devices, from_behind(): return lax.ppermute(block, axis, route)  31.6 us
    unnamed x168, local copies, waits for them, and re-layouts  31.1 us
    dot_general x4, matrix products, hidden_part(): jnp.dot(normed.reshape(-1, feat_width), up_weight, preferred_element_type...  21.6 us
  transfers between devices with their start and end apart: 16, of which 14 were waited for; matrix products, arithmetic and copies ran while one was open for 8% of the time, Pallas kernels for 0%

commit v1 on v0

v1 whole, which is shorter than its diff:
```python
import functools

import jax
import jax.numpy as jnp
import ml_dtypes
import numpy as np
from jax import lax
from jax.experimental import pallas as pl
from jax.experimental.pallas import tpu as pltpu
from jax.sharding import PartitionSpec as P

MESH = pl.DeviceIdType.MESH
F32 = jnp.float32
BF16 = jnp.bfloat16
EPSILON = 1e-05
SCALE = 0.125
ROWS, COLS = 12, 24
TOKENS = ROWS * COLS
WIN = 72
HALO = 160
PARTS = ((0, 64), (64, 64), (128, 32))


def tok_index(r, c):
    return r * COLS + c


def win_index(r, c):
    return ((r // 6) * 2 + c // 12) * WIN + (r % 6) * 12 + c % 12


def join_index(r, c):
    return (2 * (c % 2) + r % 2) * WIN + (r // 2) * 12 + c // 2


@functools.cache
def tables():
    def forward(source):
        pack = np.zeros((HALO, TOKENS), np.float32)
        own = np.zeros((TOKENS, TOKENS), np.float32)
        got = np.zeros((TOKENS, HALO), np.float32)
        for r in range(ROWS):
            for c in range(COLS):
                far_r, far_c = r + 3 >= ROWS, c + 6 >= COLS
                at = source((r + 3) % ROWS, (c + 6) % COLS)
                if not far_r and not far_c:
                    own[win_index(r, c), at] = 1
                    continue
                if far_r and not far_c:
                    slot = (r - 9) * 18 + c
                elif far_c and not far_r:
                    slot = 64 + r * 6 + (c - 18)
                else:
                    slot = 128 + (r - 9) * 6 + (c - 18)
                pack[slot, at] = 1
                got[win_index(r, c), slot] = 1
        return pack, own, got

    def back(target):
        pack = np.zeros((HALO, TOKENS), np.float32)
        own = np.zeros((TOKENS, TOKENS), np.float32)
        got = np.zeros((TOKENS, HALO), np.float32)
        for r in range(ROWS):
            for c in range(COLS):
                far_r, far_c = r < 3, c < 6
                at = win_index((r - 3) % ROWS, (c - 6) % COLS)
                if not far_r and not far_c:
                    own[target(r, c), at] = 1
                    continue
                if far_r and not far_c:
                    slot = r * 18 + (c - 6)
                elif far_c and not far_r:
                    slot = 64 + (r - 3) * 6 + c
                else:
                    slot = 128 + r * 6 + c
                pack[slot, at] = 1
                got[target(r, c), slot] = 1
        return pack, own, got

    def plain(target):
        move = np.zeros((TOKENS, TOKENS), np.float32)
        for r in range(ROWS):
            for c in range(COLS):
                move[target(r, c), tok_index(r, c)] = 1
        return move

    tok_pack, tok_own, roll_got = forward(tok_index)
    join_pack, join_own, _ = forward(join_index)
    back_pack, back_own, back_got = back(tok_index)
    _, back_own_join, back_got_join = back(join_index)
    every = (
        tok_pack, tok_own, roll_got, join_pack, join_own, back_pack, back_own, back_got,
        back_own_join, back_got_join, plain(join_index), plain(win_index),
    )
    return tuple(m.astype(ml_dtypes.bfloat16) for m in every)


def mm(a, b):
    return lax.dot_general(a, b, (((1,), (0,)), ((), ())), preferred_element_type=F32)


def mm_t(a, b):
    return lax.dot_general(a, b, (((1,), (1,)), ((), ())), preferred_element_type=F32)


def t_mm(a, b):
    return lax.dot_general(a, b, (((0,), (0,)), ((), ())), preferred_element_type=F32)


def rounded(v):
    return v.astype(BF16).astype(F32)


def standard(v):
    centred = v - jnp.mean(v, axis=-1, keepdims=True)
    scale = lax.rsqrt(jnp.mean(centred * centred, axis=-1, keepdims=True) + EPSILON)
    return centred * scale, scale


def norm_pull(grad, gain, xhat, scale):
    d = grad * gain
    return scale * (
        d - jnp.mean(d, axis=-1, keepdims=True) - xhat * jnp.mean(d * xhat, axis=-1, keepdims=True)
    )


def gelu_both(x):
    cdf = 0.5 * (1.0 + lax.erf(x * 0.7071067811865476))
    slope = cdf + x * jnp.exp(-0.5 * x * x) * 0.3989422804014327
    return x * cdf, slope


def attend(q, k, v, mask):
    e = jnp.exp(mm_t(q, k) * SCALE)
    if mask is not None:
        e = e * mask
    p = e * (1.0 / jnp.sum(e, axis=-1, keepdims=True))
    return p, mm(p.astype(BF16), v)


def attend_pull(q, k, v, p, dm):
    dv = t_mm(p.astype(BF16), dm)
    dp = rounded(mm_t(dm, v))
    ds = (p * (dp - jnp.sum(dp * p, axis=-1, keepdims=True)) * SCALE).astype(BF16)
    return mm(ds, k), t_mm(ds, q), dv


def loop(count, body):
    def step(i, carry):
        body(i)
        return carry

    lax.fori_loop(0, count, step, 0)


def chunk(i, size):
    return pl.ds(pl.multiple_of(i * size, size), size)


MERGE, TRIPLE, OUTPUT, UP, DOWN = range(5)
SLOTS = 17


class Gather:
    def __init__(self, shards, full, local_sem, send_sem, recv_sem):
        self.shards, self.full = shards, full
        self.local_sem, self.send_sem, self.recv_sem = local_sem, send_sem, recv_sem
        lat, lon = lax.axis_index("lat"), lax.axis_index("lon")
        self.z, self.xl = lat // 2, lat % 2
        self.y, self.xh, self.c = lon // 4, (lon // 2) % 2, lon % 2
        self.lat, self.lon = lat, lon
        self.up = (self.y + 1) % 4
        self.dn = (self.y + 3) % 4
        self.op = (self.y + 2) % 4
        self.copies = {}

    def place(self, z, xl, y, xh, c):
        return {"lat": z * 2 + xl, "lon": y * 4 + xh * 2 + c}

    def neighbours(self):
        z, xl, y, xh, c = self.z, self.xl, self.y, self.xh, self.c
        return [
            self.place(z, 1 - xl, y, 1 - xh, c),
            self.place(z, xl, self.up, xh, c),
            self.place(z, xl, self.dn, xh, c),
            self.place((z + 1) % 8, xl, y, xh, c),
            self.place((z + 7) % 8, xl, y, xh, c),
            self.place(z, xl, y, xh, 1 - c),
        ]

    def half(self, a):
        size = self.shards[a].shape[0] // 2
        return pl.ds(pl.multiple_of((self.z % 2) * size, size), size)

    def send(self, a, slot, src, dst, who):
        copy = pltpu.make_async_remote_copy(
            src_ref=src,
            dst_ref=dst,
            send_sem=self.send_sem.at[a, slot],
            recv_sem=self.recv_sem.at[a, slot],
            device_id=self.neighbours()[who],
            device_id_type=MESH,
        )
        copy.start()
        self.copies[a, slot] = copy

    def got(self, a, slot):
        self.copies[a, slot].wait_recv()

    def tick(self, step, a):
        shard, full, half = self.shards[a], self.full[a], self.half(a)
        y, xh, c, up, dn, op = self.y, self.xh, self.c, self.up, self.dn, self.op
        if step == 0:
            self.send(a, 0, shard, full.at[y, xh, c], 0)
            self.send(a, 1, shard.at[half], full.at[y, xh, c, half], 1)
            self.send(a, 2, shard.at[half], full.at[y, xh, c, half], 2)
            self.local = getattr(self, "local", {})
            self.local[a] = pltpu.make_async_copy(shard, full.at[y, xh, c], self.local_sem.at[a])
            self.local[a].start()
        elif step == 1:
            self.got(a, 0)
            other = full.at[y, 1 - xh, c, half]
            self.send(a, 3, other, other, 1)
            self.send(a, 4, other, other, 2)
            self.local[a].wait()
            self.send(a, 13, full.at[y, :, c], full.at[y, :, c], 5)
        elif step == 2:
            for slot, far, pick, who in ((5, dn, 0, 1), (6, up, 1, 2)):
                self.got(a, slot - 4)
                self.got(a, slot - 2)
                piece = full.at[far, pick, c, half]
                self.send(a, slot, piece, piece, who)
                base = 7 + 2 * (slot - 5)
                for d in (0, 1):
                    piece = full.at[far, d, c, half]
                    self.send(a, base + d, piece, piece, 3 + d)
        elif step == 3:
            for d in (0, 1):
                self.got(a, 5 + d)
                piece = full.at[op, d, c, half]
                self.send(a, 11 + d, piece, piece, 3 + d)
        elif step == 4:
            for i, far in enumerate((dn, up, op)):
                self.got(a, 7 + 2 * i)
                self.got(a, 8 + 2 * i)
                piece = full.at[far, :, c]
                self.send(a, 14 + i, piece, piece, 5)
        else:
            for i in range(4):
                self.got(a, 13 + i)

    def finish(self):
        for copy in self.copies.values():
            copy.wait_send()


POINTS = {
    "start": [(0, a) for a in range(5)],
    "qkv": [(1, MERGE)],
    "attention": [(2, MERGE), (1, TRIPLE)],
    "proj": [(3, MERGE), (1, OUTPUT)],
    "up": [(4, MERGE), (2, TRIPLE), (2, OUTPUT)],
    "down": [(1, UP), (3, TRIPLE), (3, OUTPUT)],
    "merge": [(5, MERGE)],
    "coarse": [(2, UP), (1, DOWN), (4, TRIPLE), (4, OUTPUT), (5, TRIPLE)],
    "coarse_out": [(3, UP), (2, DOWN), (5, OUTPUT)],
    "hidden": [(4, UP), (3, DOWN), (4, DOWN), (5, UP), (5, DOWN)],
}


def kernel(*refs):
    (
        tok, onehot, g1, wt, wo, g2, wu, wd, gm, s_merge, cg1, s_triple, s_output, cg2, s_up, s_down,
        skip_cot, coarse_cot,
        m_tok_pack, m_tok_own, m_roll_got, m_join_pack, m_join_own, m_back_pack, m_back_own, m_back_got,
        m_back_own_join, m_back_got_join, m_tok_join, m_tok_win,
        skip_out, coarse_out, grad_out,
        f_merge, f_triple, f_output, f_up, f_down,
        x_ref, n_ref, lab_ref, qkv_ref, p_ref, mix_ref, res_ref, act_ref, slope_ref, win_ref,
        grad_ref, dres_ref, dqkv_ref,
        j_ref, nj_ref, mg_ref, cn_ref, cqkv_ref, cp_ref, cmix_ref, cres_ref, cot_ref, hid_ref, dn_ref, cdqkv_ref,
        halo_send, halo_recv, local_sem, send_sem, recv_sem, halo_ssem, halo_rsem,
    ) = refs
    gather = Gather(
        (s_merge, s_triple, s_output, s_up, s_down), (f_merge, f_triple, f_output, f_up, f_down),
        local_sem, send_sem, recv_sem,
    )
    lat, lon = gather.lat, gather.lon
    north, south, west, east = (lat + 15) % 16, (lat + 1) % 16, (lon + 15) % 16, (lon + 1) % 16
    ahead = [{"lat": north, "lon": lon}, {"lat": lat, "lon": west}, {"lat": north, "lon": west}]
    behind = [{"lat": south, "lon": lon}, {"lat": lat, "lon": east}, {"lat": south, "lon": east}]
    everyone = gather.neighbours() + ahead + behind

    barrier = pltpu.get_barrier_semaphore()
    for who in everyone:
        pl.semaphore_signal(barrier, inc=1, device_id=who, device_id_type=MESH)
    pl.semaphore_wait(barrier, len(everyone))

    def point(name):
        for step, a in POINTS[name]:
            gather.tick(step, a)

    def exchange(k, value, targets):
        halo_send[k] = value.astype(BF16)
        copies = []
        for i, (first, size) in enumerate(PARTS):
            rows = pl.ds(first, size)
            copy = pltpu.make_async_remote_copy(
                src_ref=halo_send.at[k, rows],
                dst_ref=halo_recv.at[k, rows],
                send_sem=halo_ssem.at[k, i],
                recv_sem=halo_rsem.at[k, i],
                device_id=targets[i],
                device_id_type=MESH,
            )
            copy.start()
            copies.append(copy)
        return copies

    def settle(copies):
        for copy in copies:
            copy.wait()

    copies = exchange(0, mm(m_tok_pack[...], tok[...]), ahead)
    point("start")
    lab_ref[...] = mm(m_tok_win[...], onehot[...])
    x_ref[...] = mm(m_tok_own[...], tok[...])
    settle(copies)
    x_ref[...] += mm(m_roll_got[...], halo_recv[0])

    def first_norm(i):
        rows = chunk(i, 96)
        n_ref[rows] = (standard(x_ref[rows])[0] * g1[...]).astype(BF16)

    loop(3, first_norm)

    def project(i):
        cols = chunk(i, 256)
        qkv_ref[:, cols] = rounded(mm(n_ref[...], wt[:, cols]))

    loop(6, project)
    point("qkv")

    def fine_attention(w):
        rows = chunk(w, WIN)
        seen = lab_ref[rows].astype(BF16)
        mask = mm_t(seen, seen)
        for pair in range(4):
            mixed = []
            for h in (2 * pair, 2 * pair + 1):
                q, k, v = (
                    qkv_ref[rows, h * 192 + 64 * i : h * 192 + 64 * i + 64].astype(BF16) for i in range(3)
                )
                p, m = attend(q, k, v, mask)
                p_ref[w * 8 + h] = p
                mixed.append(m)
            mix_ref[rows, pair * 128 : pair * 128 + 128] = jnp.concatenate(mixed, axis=-1)

    loop(4, fine_attention)
    point("attention")

    def out_project(i):
        cols = chunk(i, 256)
        res_ref[:, cols] = x_ref[:, cols] + mm(mix_ref[...].astype(BF16), wo[:, cols])

    loop(2, out_project)

    def second_norm(i):
        rows = chunk(i, 96)
        n_ref[rows] = (standard(res_ref[rows])[0] * g2[...]).astype(BF16)

    loop(3, second_norm)
    point("proj")

    def lift(i):
        cols = chunk(i, 256)
        active, slope = gelu_both(mm(n_ref[...], wu[:, cols]))
        act_ref[:, cols] = active.astype(BF16)
        slope_ref[:, cols] = slope.astype(BF16)

    loop(8, lift)
    point("up")

    def lower(i):
        cols = chunk(i, 256)
        win_ref[:, cols] = (res_ref[:, cols] + mm(act_ref[...], wd[:, cols])).astype(BF16)

    loop(2, lower)
    copies = exchange(1, mm(m_back_pack[...], win_ref[...]), behind)
    point("down")
    j_ref[...] = mm(m_back_own_join[...], win_ref[...])
    x_kept = mm(m_back_own[...], win_ref[...])
    settle(copies)
    j_ref[...] += mm(m_back_got_join[...], halo_recv[1])
    skip_out[...] = (x_kept + mm(m_back_got[...], halo_recv[1])).astype(BF16)

    quads = [pl.ds(q * WIN, WIN) for q in range(4)]

    def joined_standard():
        average = sum(jnp.sum(j_ref[q], axis=-1, keepdims=True) for q in quads) * (1.0 / 2048)
        square = 0.0
        for q in quads:
            centred = j_ref[q] - average
            square = square + jnp.sum(centred * centred, axis=-1, keepdims=True)
        return average, lax.rsqrt(square * (1.0 / 2048) + EPSILON)

    average, merge_scale = joined_standard()
    for i, q in enumerate(quads):
        nj_ref[:, i * 512 : i * 512 + 512] = (
            (j_ref[q] - average) * merge_scale * gm[:, i * 512 : i * 512 + 512]
        ).astype(BF16)
    for i in range(6):
        cot_ref[i * 12 : i * 12 + 12] = coarse_cot[i].astype(F32)
    point("merge")

    def merge(i):
        cols = chunk(i, 256)
        weight = f_merge[:, :, :, :, cols].reshape(2048, 256)
        mg_ref[:, cols] = rounded(mm(nj_ref[...], weight))

    loop(4, merge)

    xhat, scale = standard(mg_ref[...])
    cn_ref[...] = (xhat * cg1[...]).astype(BF16)
    point("coarse")

    def coarse_attention(y):
        mixed = []
        for i in range(4):
            part = mm(cn_ref[...], f_triple[y, i // 2, i % 2]).astype(BF16)
            cqkv_ref[y * 4 + i] = part.astype(F32)
            p, m = attend(part[:, :64], part[:, 64:128], part[:, 128:], None)
            cp_ref[y * 4 + i] = p
            mixed.append(m)
        cmix_ref[:, chunk(y, 256)] = jnp.concatenate(mixed, axis=-1).astype(BF16)

    loop(4, coarse_attention)
    point("coarse_out")

    def coarse_project(i):
        cols = chunk(i, 256)
        weight = f_output[:, :, :, :, cols].reshape(1024, 256)
        cres_ref[:, cols] = mg_ref[:, cols] + mm(cmix_ref[...], weight)

    loop(4, coarse_project)
    xhat, scale = standard(cres_ref[...])
    cn_ref[...] = (xhat * cg2[...]).astype(BF16)
    hid_ref[...] = cres_ref[...]
    dn_ref[...] = jnp.zeros_like(dn_ref)
    point("hidden")

    def coarse_hidden(y):
        for i in range(4):
            upper, lower_weight = f_up[y, i // 2, i % 2], f_down[y, i // 2, i % 2]
            active, slope = gelu_both(mm(cn_ref[...], upper))
            hid_ref[...] += mm(active.astype(BF16), lower_weight)
            grad = rounded(mm_t(cot_ref[...].astype(BF16), lower_weight))
            dn_ref[...] += mm_t((grad * slope).astype(BF16), upper)

    loop(4, coarse_hidden)
    for i in range(6):
        coarse_out[i] = hid_ref[i * 12 : i * 12 + 12].astype(BF16)
    xhat, scale = standard(cres_ref[...])
    cres_ref[...] = cot_ref[...] + norm_pull(dn_ref[...], cg2[...], xhat, scale)

    def coarse_mix_pull(i):
        rows_of = f_output[i].reshape(256, 1024)
        cmix_ref[:, chunk(i, 256)] = mm_t(cres_ref[...].astype(BF16), rows_of).astype(BF16)

    loop(4, coarse_mix_pull)
    dn_ref[...] = jnp.zeros_like(dn_ref)

    def coarse_attention_pull(y):
        dmix = cmix_ref[:, chunk(y, 256)]
        for i in range(4):
            part = cqkv_ref[y * 4 + i].astype(BF16)
            dq, dk, dv = attend_pull(
                part[:, :64], part[:, 64:128], part[:, 128:], cp_ref[y * 4 + i], dmix[:, i * 64 : i * 64 + 64]
            )
            packed = jnp.concatenate([dq, dk, dv], axis=-1).astype(BF16)
            dn_ref[...] += mm_t(packed, f_triple[y, i // 2, i % 2])

    loop(4, coarse_attention_pull)
    xhat, scale = standard(mg_ref[...])
    cn_ref[...] = (cres_ref[...] + norm_pull(dn_ref[...], cg1[...], xhat, scale)).astype(BF16)

    def merge_pull(y):
        res_rows = chunk(y, WIN)
        grad_ref[res_rows] = rounded(mm_t(cn_ref[...], f_merge[y].reshape(512, 1024)))

    loop(4, merge_pull)
    first = 0.0
    second = 0.0
    for i, q in enumerate(quads):
        d = grad_ref[q] * gm[:, i * 512 : i * 512 + 512]
        first = first + jnp.sum(d, axis=-1, keepdims=True)
        second = second + jnp.sum(d * (j_ref[q] - average), axis=-1, keepdims=True)
    first = first * (1.0 / 2048)
    second = second * merge_scale * (1.0 / 2048)
    dqkv_ref[:, :512] = mm(m_tok_join[...], skip_cot[...])
    for i, q in enumerate(quads):
        d = grad_ref[q] * gm[:, i * 512 : i * 512 + 512]
        xhat = (j_ref[q] - average) * merge_scale
        grad_ref[q] = dqkv_ref[q, :512] + merge_scale * (d - first - xhat * second)

    win_ref[...] = grad_ref[...].astype(BF16)
    copies = exchange(2, mm(m_join_pack[...], win_ref[...]), ahead)
    grad_ref[...] = mm(m_join_own[...], win_ref[...])
    settle(copies)
    grad_ref[...] += mm(m_roll_got[...], halo_recv[2])

    def lower_pull(i):
        cols = chunk(i, 256)
        grad = rounded(mm_t(grad_ref[...].astype(BF16), wd[cols]))
        act_ref[:, cols] = (grad * slope_ref[:, cols].astype(F32)).astype(BF16)

    loop(8, lower_pull)

    def lift_pull(i):
        rows = chunk(i, 256)
        dres_ref[:, rows] = rounded(mm_t(act_ref[...], wu[rows]))

    loop(2, lift_pull)

    def second_pull(i):
        rows = chunk(i, 96)
        xhat, scale = standard(res_ref[rows])
        total = grad_ref[rows] + norm_pull(dres_ref[rows], g2[...], xhat, scale)
        dres_ref[rows] = total
        n_ref[rows] = total.astype(BF16)

    loop(3, second_pull)

    def out_pull(i):
        rows = chunk(i, 256)
        mix_ref[:, rows] = rounded(mm_t(n_ref[...], wo[rows]))

    loop(2, out_pull)

    def fine_attention_pull(w):
        rows = chunk(w, WIN)
        for pair in range(4):
            packed = []
            for h in (2 * pair, 2 * pair + 1):
                q, k, v = (
                    qkv_ref[rows, h * 192 + 64 * i : h * 192 + 64 * i + 64].astype(BF16) for i in range(3)
                )
                dm = mix_ref[rows, h * 64 : h * 64 + 64].astype(BF16)
                packed.extend(attend_pull(q, k, v, p_ref[w * 8 + h], dm))
            dqkv_ref[rows, pair * 384 : pair * 384 + 384] = jnp.concatenate(packed, axis=-1)

    loop(4, fine_attention_pull)

    def project_pull(i):
        rows = chunk(i, 256)
        grad_ref[:, rows] = rounded(mm_t(dqkv_ref[...].astype(BF16), wt[rows]))

    loop(2, project_pull)

    def first_pull(i):
        rows = chunk(i, 96)
        xhat, scale = standard(x_ref[rows])
        win_ref[rows] = (dres_ref[rows] + norm_pull(grad_ref[rows], g1[...], xhat, scale)).astype(BF16)

    loop(3, first_pull)
    copies = exchange(3, mm(m_back_pack[...], win_ref[...]), behind)
    grad_ref[...] = mm(m_back_own[...], win_ref[...])
    gather.finish()
    settle(copies)
    grad_out[...] = (grad_ref[...] + mm(m_back_got[...], halo_recv[3])).astype(BF16)


def local(
    fine_tokens, region_labels, g1, wt, wo, g2, wu, wd, gm, s_merge, cg1, s_triple, s_output, cg2, s_up, s_down,
    skip_cot, coarse_cot,
):
    onehot = (region_labels.reshape(TOKENS, 1) == jnp.arange(128, dtype=jnp.int32)[None]).astype(BF16)
    moves = [jnp.asarray(m) for m in tables()]
    vmem = pl.BlockSpec(memory_space=pltpu.VMEM)
    held = pl.BlockSpec(memory_space=pl.ANY)
    shards = (s_merge, s_triple, s_output, s_up, s_down)
    args = [
        fine_tokens.reshape(TOKENS, 512), onehot, g1[None], wt, wo, g2[None], wu, wd, gm[None], s_merge, cg1[None],
        s_triple, s_output, cg2[None], s_up, s_down, skip_cot.reshape(TOKENS, 512), coarse_cot, *moves,
    ]
    in_specs = [held if any(a is s for s in shards) else vmem for a in args]
    f32 = lambda *shape: pltpu.VMEM(shape, F32)
    bf16 = lambda *shape: pltpu.VMEM(shape, BF16)
    scratch = [bf16(4, 2, 2, *s.shape) for s in shards]
    scratch += [
        f32(288, 512), bf16(288, 512), f32(288, 128), f32(288, 1536), f32(32, 72, 72), f32(288, 512),
        f32(288, 512), bf16(288, 2048), bf16(288, 2048), bf16(288, 512),
        f32(288, 512), f32(288, 512), f32(288, 1536),
        f32(288, 512), bf16(72, 2048), f32(72, 1024), bf16(72, 1024), f32(16, 72, 192), f32(16, 72, 72),
        bf16(72, 1024), f32(72, 1024), f32(72, 1024), f32(72, 1024), f32(72, 1024), f32(8, 128),
        bf16(4, HALO, 512), bf16(4, HALO, 512),
        pltpu.SemaphoreType.DMA((5,)), pltpu.SemaphoreType.DMA((5, SLOTS)), pltpu.SemaphoreType.DMA((5, SLOTS)),
        pltpu.SemaphoreType.DMA((4, 3)), pltpu.SemaphoreType.DMA((4, 3)),
    ]
    skip, coarse, grad = pl.pallas_call(
        kernel,
        out_shape=[
            jax.ShapeDtypeStruct((TOKENS, 512), BF16),
            jax.ShapeDtypeStruct((6, 12, 1024), BF16),
            jax.ShapeDtypeStruct((TOKENS, 512), BF16),
        ],
        in_specs=in_specs,
        out_specs=[vmem] * 3,
        scratch_shapes=scratch,
        compiler_params=pltpu.CompilerParams(
            collective_id=0, has_side_effects=True, vmem_limit_bytes=60 * 1024 * 1024
        ),
        name="backbone",
    )(*args)
    return skip.reshape(ROWS, COLS, 512), coarse, grad.reshape(ROWS, COLS, 512)


def solution(mesh):
    in_specs = (
        P("lat", "lon", None), P("lat", "lon"), P(), P(), P(), P(), P(), P(), P(), P("lon", None), P(),
        P(None, "lon"), P("lon", None), P(), P(None, "lon"), P("lon", None),
        P("lat", "lon", None), P("lat", "lon", None),
    )
    out_specs = (P("lat", "lon", None), P("lat", "lon", None), P("lat", "lon", None))
    return jax.shard_map(local, mesh=mesh, in_specs=in_specs, out_specs=out_specs, check_vma=False)
```

time: 1000 us -> 176 us (0.18); the launches traced: 985 us -> 176 us
  waiting for transfers between devices: 695 us -> 0 us
  Pallas kernels: 0 us -> 167 us
  local copies, waits for them, and re-layouts: 150 us -> 7.76 us
  matrix products: 67.6 us -> 0 us
  other arithmetic: 40 us -> 0.74 us
  starting transfers between devices: 15.8 us -> 0 us
  between operations: 16.4 us -> 0.64 us
    unnamed x11 -> x0, waiting for transfers between devices: 442 us -> none
    all_gather x5 -> x0, waiting for transfers between devices: 222 us -> none  [the longest x1 59.8 us: local(): cotangent_band = lax.all_gather(coarse_cotangent, 'lon', axis=1, tiled=True)]
    pallas_call x0 -> x1, Pallas kernels: none -> 167 us  [local(): pl.pallas_call(kernel, out_shape=[jax.ShapeDtypeStruct((TOKENS, 512), BF1...]
    dot_general x28 -> x0, matrix products: 67.6 us -> none  [the longest x4 21.6 us: hidden_part(): jnp.dot(normed.reshape(-1, feat_width), up_weight, preferred_element_type...]
    reshape x17 -> x0, local copies, waits for them, and re-layouts: 36.6 us -> none  [the longest x2 9.21 us: window_attention(): packed = packed.reshape(window_count, window_size, head_count, 3, head_size)]
    ppermute x8 -> x0, waiting for transfers between devices: 31.6 us -> none  [from_behind(): return lax.ppermute(block, axis, route)]
    unnamed x168 -> x4, local copies, waits for them, and re-layouts: 31.1 us -> 6.99 us
    transpose x11 -> x0, local copies, waits for them, and re-layouts: 18.4 us -> none  [the longest x4 8.7 us: to_windows(): blocks = blocks.transpose(0, 2, 1, 3, 4)]
  transfers between devices with their start and end apart: 16 -> 0, of which waited for: 14 -> 0; matrix products, arithmetic and copies ran while one was open for 8% -> 0% of each run, Pallas kernels for 0% -> 0%
where the time goes in v1:
time: 176 us
  Pallas kernels  167 us (95%)
  local copies, waits for them, and re-layouts  7.76 us (4%)
    pallas_call x1, Pallas kernels, local(): pl.pallas_call(kernel, out_shape=[jax.ShapeDtypeStruct((TOKENS, 512), BF1...  167 us
    unnamed x4, local copies, waits for them, and re-layouts  6.99 us

profile of v1, /device:TPU:8, one launch (start us, length us, event | category | flops | bytes accessed | tf_op | source)
XLA Modules:
  0.0 176.1 jit_solution(2288689495710337761)
XLA Ops:
  0.6 0.8 eq.15
  1.4 0.7 fusion.refs_1_
  2.2 2.0 %copy.33.refs_11_ = bf16[1024,192]{1,0:T(8,128)(2,1)} copy(bf16[1024,192]{0,1:T(8,128)(2,1)} %param.41) | data formatting | bytes 786432 | tf_op args[11]
  4.1 167.0 %backbone.1 = (bf16[288,512]{1,0:T(8,128)(2,1)}, bf16[6,12,1024]{2,1,0:T(8,128)(2,1)}, bf16[288,512]{1,0:T(8,128)(2,1)}) custom-call(bf16[288,512]{1,0:T(8,128)(2,1)} %bitcast.9, bf16[288,128]{1,0:T(8,128)(2,1)} %fusion.refs_1_, f32[1,512]{1,0:T(1,128)} %bitcast.16, bf16[512,1536]{1,0:T(8,128)(2,1)} %refs_3_.1, bf16[512,512]{1,0:T(8,128)(2,1)} %refs_4_.1, ...), custom_call_target="tpu_custom_call" | custom-call | tf_op jit(solution)/shard_map/backbone/pallas_call | solution.py:600
  171.1 1.7 copy.37
  172.8 1.6 copy.38
  174.4 1.7 copy.39

commit v2 on v1

--- a/solution.py
+++ b/solution.py
@@ -173,6 +173,13 @@
         self.dn = (self.y + 3) % 4
         self.op = (self.y + 2) % 4
         self.copies = {}
+        self.local = {}
+
+    def begin(self):
+        for a in range(5):
+            here = self.full[a].at[self.y, self.xh, self.c]
+            self.local[a] = pltpu.make_async_copy(self.shards[a], here, self.local_sem.at[a])
+            self.local[a].start()
 
     def place(self, z, xl, y, xh, c):
         return {"lat": z * 2 + xl, "lon": y * 4 + xh * 2 + c}
@@ -208,21 +215,19 @@
         self.copies[a, slot].wait_recv()
 
     def tick(self, step, a):
-        shard, full, half = self.shards[a], self.full[a], self.half(a)
+        full, half = self.full[a], self.half(a)
         y, xh, c, up, dn, op = self.y, self.xh, self.c, self.up, self.dn, self.op
         if step == 0:
-            self.send(a, 0, shard, full.at[y, xh, c], 0)
-            self.send(a, 1, shard.at[half], full.at[y, xh, c, half], 1)
-            self.send(a, 2, shard.at[half], full.at[y, xh, c, half], 2)
-            self.local = getattr(self, "local", {})
-            self.local[a] = pltpu.make_async_copy(shard, full.at[y, xh, c], self.local_sem.at[a])
-            self.local[a].start()
+            self.local[a].wait()
+            self.send(a, 0, full.at[y, xh, c], full.at[y, xh, c], 0)
+            piece = full.at[y, xh, c, half]
+            self.send(a, 1, piece, piece, 1)
+            self.send(a, 2, piece, piece, 2)
         elif step == 1:
             self.got(a, 0)
             other = full.at[y, 1 - xh, c, half]
             self.send(a, 3, other, other, 1)
             self.send(a, 4, other, other, 2)
-            self.local[a].wait()
             self.send(a, 13, full.at[y, :, c], full.at[y, :, c], 5)
         elif step == 2:
             for slot, far, pick, who in ((5, dn, 0, 1), (6, up, 1, 2)):
@@ -239,38 +244,42 @@
                 self.got(a, 5 + d)
                 piece = full.at[op, d, c, half]
                 self.send(a, 11 + d, piece, piece, 3 + d)
-        elif step == 4:
-            for i, far in enumerate((dn, up, op)):
+        elif step in (4, 5):
+            for i, far in (((0, dn), (1, up)), ((2, op),))[step - 4]:
                 self.got(a, 7 + 2 * i)
                 self.got(a, 8 + 2 * i)
                 piece = full.at[far, :, c]
                 self.send(a, 14 + i, piece, piece, 5)
         else:
-            for i in range(4):
-                self.got(a, 13 + i)
+            self.got(a, 13 + step - 6)
 
     def finish(self):
         for copy in self.copies.values():
             copy.wait_send()
 
 
+M, T, O, U, D = range(5)
 POINTS = {
-    "start": [(0, a) for a in range(5)],
-    "qkv": [(1, MERGE)],
-    "attention": [(2, MERGE), (1, TRIPLE)],
-    "proj": [(3, MERGE), (1, OUTPUT)],
-    "up": [(4, MERGE), (2, TRIPLE), (2, OUTPUT)],
-    "down": [(1, UP), (3, TRIPLE), (3, OUTPUT)],
-    "merge": [(5, MERGE)],
-    "coarse": [(2, UP), (1, DOWN), (4, TRIPLE), (4, OUTPUT), (5, TRIPLE)],
-    "coarse_out": [(3, UP), (2, DOWN), (5, OUTPUT)],
-    "hidden": [(4, UP), (3, DOWN), (4, DOWN), (5, UP), (5, DOWN)],
+    "start": [(0, M), (0, O), (0, T), (0, U)],
+    "rolled": [(1, M), (1, O)],
+    "attention": [(2, M)],
+    "down": [(0, D), (1, T), (2, O), (4, M), (3, M)],
+    "merge": [(4, O), (2, T), (5, M), (3, O), (6, M), (7, M), (8, M), (9, M)],
+    "coarse": [(1, U), (3, T), (6, T)],
+    "coarse 1": [(4, T), (7, T), (8, T)],
+    "coarse 2": [(5, O), (2, U), (1, D), (5, T)],
+    "coarse 3": [(9, T)],
+    "coarse out": [(3, U), (6, O), (7, O), (8, O), (9, O)],
+    "hidden": [(4, U), (2, D), (6, U), (6, D)],
+    "hidden 1": [(5, U), (3, D), (4, D), (7, U), (7, D)],
+    "hidden 2": [(5, D), (8, U), (8, D)],
+    "hidden 3": [(9, U), (9, D)],
 }
 
 
 def kernel(*refs):
     (
-        tok, onehot, g1, wt, wo, g2, wu, wd, gm, s_merge, cg1, s_triple, s_output, cg2, s_up, s_down,
+        tok, label_row, g1, wt, wo, g2, wu, wd, gm, s_merge, cg1, s_triple, s_output, cg2, s_up, s_down,
         skip_cot, coarse_cot,
         m_tok_pack, m_tok_own, m_roll_got, m_join_pack, m_join_own, m_back_pack, m_back_own, m_back_got,
         m_back_own_join, m_back_got_join, m_tok_join, m_tok_win,
@@ -291,6 +300,7 @@
     behind = [{"lat": south, "lon": lon}, {"lat": lat, "lon": east}, {"lat": south, "lon": east}]
     everyone = gather.neighbours() + ahead + behind
 
+    gather.begin()
     barrier = pltpu.get_barrier_semaphore()
     for who in everyone:
         pl.semaphore_signal(barrier, inc=1, device_id=who, device_id_type=MESH)
@@ -323,8 +333,10 @@
 
     copies = exchange(0, mm(m_tok_pack[...], tok[...]), ahead)
     point("start")
-    lab_ref[...] = mm(m_tok_win[...], onehot[...])
+    each = lax.broadcasted_iota(jnp.int32, (8, TOKENS), 0)
+    lab_ref[...] = mm_t(m_tok_win[...], jnp.where(each == label_row[...], 1.0, 0.0).astype(BF16))
     x_ref[...] = mm(m_tok_own[...], tok[...])
+    point("rolled")
     settle(copies)
     x_ref[...] += mm(m_roll_got[...], halo_recv[0])
 
@@ -339,7 +351,6 @@
         qkv_ref[:, cols] = rounded(mm(n_ref[...], wt[:, cols]))
 
     loop(6, project)
-    point("qkv")
 
     def fine_attention(w):
         rows = chunk(w, WIN)
@@ -370,7 +381,6 @@
         n_ref[rows] = (standard(res_ref[rows])[0] * g2[...]).astype(BF16)
 
     loop(3, second_norm)
-    point("proj")
 
     def lift(i):
         cols = chunk(i, 256)
@@ -379,7 +389,6 @@
         slope_ref[:, cols] = slope.astype(BF16)
 
     loop(8, lift)
-    point("up")
 
     def lower(i):
         cols = chunk(i, 256)
@@ -422,20 +431,23 @@
 
     xhat, scale = standard(mg_ref[...])
     cn_ref[...] = (xhat * cg1[...]).astype(BF16)
-    point("coarse")
+    order = (gather.y, gather.dn, gather.up, gather.op)
 
     def coarse_attention(y):
         mixed = []
+        packed = mm_t(cn_ref[...], f_triple[y].reshape(768, 1024))
+        cqkv_ref[y] = packed
         for i in range(4):
-            part = mm(cn_ref[...], f_triple[y, i // 2, i % 2]).astype(BF16)
-            cqkv_ref[y * 4 + i] = part.astype(F32)
+            part = packed[:, i * 192 : i * 192 + 192].astype(BF16)
             p, m = attend(part[:, :64], part[:, 64:128], part[:, 128:], None)
             cp_ref[y * 4 + i] = p
             mixed.append(m)
         cmix_ref[:, chunk(y, 256)] = jnp.concatenate(mixed, axis=-1).astype(BF16)
 
-    loop(4, coarse_attention)
-    point("coarse_out")
+    for name, y in zip(("coarse", "coarse 1", "coarse 2", "coarse 3"), order):
+        point(name)
+        coarse_attention(y)
+    point("coarse out")
 
     def coarse_project(i):
         cols = chunk(i, 256)
@@ -447,17 +459,23 @@
     cn_ref[...] = (xhat * cg2[...]).astype(BF16)
     hid_ref[...] = cres_ref[...]
     dn_ref[...] = jnp.zeros_like(dn_ref)
-    point("hidden")
 
     def coarse_hidden(y):
+        lower_weight = f_down[y].reshape(1024, 1024)
+        grad = rounded(mm_t(cot_ref[...].astype(BF16), lower_weight))
+        active = []
+        total = dn_ref[...]
         for i in range(4):
-            upper, lower_weight = f_up[y, i // 2, i % 2], f_down[y, i // 2, i % 2]
-            active, slope = gelu_both(mm(cn_ref[...], upper))
-            hid_ref[...] += mm(active.astype(BF16), lower_weight)
-            grad = rounded(mm_t(cot_ref[...].astype(BF16), lower_weight))
-            dn_ref[...] += mm_t((grad * slope).astype(BF16), upper)
-
-    loop(4, coarse_hidden)
+            upper = f_up[y, i // 2, i % 2]
+            value, slope = gelu_both(mm(cn_ref[...], upper))
+            active.append(value.astype(BF16))
+            total = total + mm_t((grad[:, i * 256 : i * 256 + 256] * slope).astype(BF16), upper)
+        dn_ref[...] = total
+        hid_ref[...] += mm(jnp.concatenate(active, axis=-1), lower_weight)
+
+    for name, y in zip(("hidden", "hidden 1", "hidden 2", "hidden 3"), order):
+        point(name)
+        coarse_hidden(y)
     for i in range(6):
         coarse_out[i] = hid_ref[i * 12 : i * 12 + 12].astype(BF16)
     xhat, scale = standard(cres_ref[...])
@@ -472,13 +490,16 @@
 
     def coarse_attention_pull(y):
         dmix = cmix_ref[:, chunk(y, 256)]
+        packed = []
         for i in range(4):
-            part = cqkv_ref[y * 4 + i].astype(BF16)
-            dq, dk, dv = attend_pull(
-                part[:, :64], part[:, 64:128], part[:, 128:], cp_ref[y * 4 + i], dmix[:, i * 64 : i * 64 + 64]
+            part = cqkv_ref[y, :, i * 192 : i * 192 + 192].astype(BF16)
+            packed.extend(
+                attend_pull(
+                    part[:, :64], part[:, 64:128], part[:, 128:], cp_ref[y * 4 + i], dmix[:, i * 64 : i * 64 + 64]
+                )
             )
-            packed = jnp.concatenate([dq, dk, dv], axis=-1).astype(BF16)
-            dn_ref[...] += mm_t(packed, f_triple[y, i // 2, i % 2])
+        packed = jnp.concatenate(packed, axis=-1).astype(BF16)
+        dn_ref[...] += mm(packed, f_triple[y].reshape(768, 1024))
 
     loop(4, coarse_attention_pull)
     xhat, scale = standard(mg_ref[...])
@@ -570,17 +591,23 @@
     grad_out[...] = (grad_ref[...] + mm(m_back_got[...], halo_recv[3])).astype(BF16)
 
 
+def place_results(*refs):
+    for i in range(3):
+        refs[3 + i][...] = refs[i][...]
+
+
 def local(
     fine_tokens, region_labels, g1, wt, wo, g2, wu, wd, gm, s_merge, cg1, s_triple, s_output, cg2, s_up, s_down,
     skip_cot, coarse_cot,
 ):
-    onehot = (region_labels.reshape(TOKENS, 1) == jnp.arange(128, dtype=jnp.int32)[None]).astype(BF16)
+    label_row = region_labels.reshape(1, TOKENS)
     moves = [jnp.asarray(m) for m in tables()]
     vmem = pl.BlockSpec(memory_space=pltpu.VMEM)
     held = pl.BlockSpec(memory_space=pl.ANY)
+    s_triple = s_triple.T
     shards = (s_merge, s_triple, s_output, s_up, s_down)
     args = [
-        fine_tokens.reshape(TOKENS, 512), onehot, g1[None], wt, wo, g2[None], wu, wd, gm[None], s_merge, cg1[None],
+        fine_tokens.reshape(TOKENS, 512), label_row, g1[None], wt, wo, g2[None], wu, wd, gm[None], s_merge, cg1[None],
         s_triple, s_output, cg2[None], s_up, s_down, skip_cot.reshape(TOKENS, 512), coarse_cot, *moves,
     ]
     in_specs = [held if any(a is s for s in shards) else vmem for a in args]
@@ -588,10 +615,10 @@
     bf16 = lambda *shape: pltpu.VMEM(shape, BF16)
     scratch = [bf16(4, 2, 2, *s.shape) for s in shards]
     scratch += [
-        f32(288, 512), bf16(288, 512), f32(288, 128), f32(288, 1536), f32(32, 72, 72), f32(288, 512),
+        f32(288, 512), bf16(288, 512), f32(288, 8), f32(288, 1536), f32(32, 72, 72), f32(288, 512),
         f32(288, 512), bf16(288, 2048), bf16(288, 2048), bf16(288, 512),
         f32(288, 512), f32(288, 512), f32(288, 1536),
-        f32(288, 512), bf16(72, 2048), f32(72, 1024), bf16(72, 1024), f32(16, 72, 192), f32(16, 72, 72),
+        f32(288, 512), bf16(72, 2048), f32(72, 1024), bf16(72, 1024), f32(4, 72, 768), f32(16, 72, 72),
         bf16(72, 1024), f32(72, 1024), f32(72, 1024), f32(72, 1024), f32(72, 1024), f32(8, 128),
         bf16(4, HALO, 512), bf16(4, HALO, 512),
         pltpu.SemaphoreType.DMA((5,)), pltpu.SemaphoreType.DMA((5, SLOTS)), pltpu.SemaphoreType.DMA((5, SLOTS)),
@@ -612,6 +639,13 @@
         ),
         name="backbone",
     )(*args)
+    skip, coarse, grad = pl.pallas_call(
+        place_results,
+        out_shape=[jax.ShapeDtypeStruct(a.shape, a.dtype) for a in (skip, coarse, grad)],
+        in_specs=[vmem] * 3,
+        out_specs=[vmem] * 3,
+        name="results",
+    )(skip, coarse, grad)
     return skip.reshape(ROWS, COLS, 512), coarse, grad.reshape(ROWS, COLS, 512)
 
 

time: 176 us -> 150 us (0.85)
  Pallas kernels: 167 us -> 147 us
  local copies, waits for them, and re-layouts: 7.76 us -> 1.34 us
    pallas_call x1, Pallas kernels: 167 us -> 145 us  [local(): pl.pallas_call(kernel, out_shape=[jax.ShapeDtypeStruct((TOKENS, 512), BF1...]
    unnamed x4 -> x0, local copies, waits for them, and re-layouts: 6.99 us -> none
    pallas_call x0 -> x1, Pallas kernels: none -> 2.05 us  [local(): pl.pallas_call(place_results, out_shape=[jax.ShapeDtypeStruct(a.shape, a....]
where the time goes in v2:
time: 150 us; the launch traced here: 149 us
  Pallas kernels  147 us (98%)
    pallas_call x1, Pallas kernels, local(): pl.pallas_call(kernel, out_shape=[jax.ShapeDtypeStruct((TOKENS, 512), BF1...  145 us

profile of v2, /device:TPU:8, one launch (start us, length us, event | category | flops | bytes accessed | tf_op | source)
XLA Modules:
  0.0 149.0 jit_solution(12402939419729932643)
XLA Ops:
  0.6 1.3 reshape.22.refs_1_
  2.0 144.9 %backbone.1 = (bf16[288,512]{1,0:T(8,128)(2,1)}, bf16[6,12,1024]{2,1,0:T(8,128)(2,1)}, bf16[288,512]{1,0:T(8,128)(2,1)}) custom-call(bf16[288,512]{1,0:T(8,128)(2,1)} %bitcast.11, s32[1,288]{1,0:T(1,128)} %reshape.22.refs_1_, f32[1,512]{1,0:T(1,128)} %bitcast.16, bf16[512,1536]{1,0:T(8,128)(2,1)} %refs_3_.1, bf16[512,512]{1,0:T(8,128)(2,1)} %refs_4_.1, ...), custom_call_target="tpu_custom_call" | custom-call | tf_op jit(solution)/shard_map/backbone/pallas_call | solution.py:627
  146.9 2.0 %results.1 = (bf16[288,512]{1,0:T(8,128)(2,1)}, bf16[6,12,1024]{2,1,0:T(8,128)(2,1)}, bf16[288,512]{1,0:T(8,128)(2,1)}) custom-call(bf16[288,512]{1,0:T(8,128)(2,1)} %get-tuple-element.9.refs_0_, bf16[6,12,1024]{2,1,0:T(8,128)(2,1)} %get-tuple-element.10.refs_1_, bf16[288,512]{1,0:T(8,128)(2,1)} %get-tuple-element.11.refs_2_), custom_call_target="tpu_custom_call" | custom-call | tf_op jit(solution)/shard_map/results/pallas_call | solution.py:642

commit v3 on v2

--- a/solution.py
+++ b/solution.py
@@ -103,10 +103,6 @@
     return lax.dot_general(a, b, (((1,), (1,)), ((), ())), preferred_element_type=F32)
 
 
-def t_mm(a, b):
-    return lax.dot_general(a, b, (((0,), (0,)), ((), ())), preferred_element_type=F32)
-
-
 def rounded(v):
     return v.astype(BF16).astype(F32)
 
@@ -131,18 +127,20 @@
 
 
 def attend(q, k, v, mask):
-    e = jnp.exp(mm_t(q, k) * SCALE)
+    e, turned = jnp.exp(mm_t(q, k) * SCALE), jnp.exp(mm_t(k, q) * SCALE)
     if mask is not None:
-        e = e * mask
+        e, turned = e * mask, turned * mask
     p = e * (1.0 / jnp.sum(e, axis=-1, keepdims=True))
-    return p, mm(p.astype(BF16), v)
-
-
-def attend_pull(q, k, v, p, dm):
-    dv = t_mm(p.astype(BF16), dm)
-    dp = rounded(mm_t(dm, v))
-    ds = (p * (dp - jnp.sum(dp * p, axis=-1, keepdims=True)) * SCALE).astype(BF16)
-    return mm(ds, k), t_mm(ds, q), dv
+    turned = turned * (1.0 / jnp.sum(turned, axis=0, keepdims=True))
+    return p, turned, mm(p.astype(BF16), v)
+
+
+def attend_pull(q, k, v, p, turned, dm):
+    dv = mm(turned.astype(BF16), dm)
+    dp, dp_turned = rounded(mm_t(dm, v)), rounded(mm_t(v, dm))
+    ds = p * (dp - jnp.sum(dp * p, axis=-1, keepdims=True)) * SCALE
+    ds_turned = turned * (dp_turned - jnp.sum(dp_turned * turned, axis=0, keepdims=True)) * SCALE
+    return mm(ds.astype(BF16), k), mm(ds_turned.astype(BF16), q), dv
 
 
 def loop(count, body):
@@ -158,7 +156,8 @@
 
 
 MERGE, TRIPLE, OUTPUT, UP, DOWN = range(5)
-SLOTS = 17
+SLOTS = 21
+QUARTERED = (TRIPLE, OUTPUT)
 
 
 class Gather:
@@ -193,11 +192,18 @@
             self.place((z + 1) % 8, xl, y, xh, c),
             self.place((z + 7) % 8, xl, y, xh, c),
             self.place(z, xl, y, xh, 1 - c),
+            self.place(z, 1 - xl, y, xh, c),
         ]
 
-    def half(self, a):
+    def half(self, a, which):
         size = self.shards[a].shape[0] // 2
-        return pl.ds(pl.multiple_of((self.z % 2) * size, size), size)
+        return pl.ds(pl.multiple_of(which * size, size), size)
+
+    def share(self, a):
+        if a not in QUARTERED:
+            return self.half(a, self.z % 2)
+        size = self.shards[a].shape[0] // 4
+        return pl.ds(pl.multiple_of((self.xl * 2 + self.z % 2) * size, size), size)
 
     def send(self, a, slot, src, dst, who):
         copy = pltpu.make_async_remote_copy(
@@ -215,16 +221,21 @@
         self.copies[a, slot].wait_recv()
 
     def tick(self, step, a):
-        full, half = self.full[a], self.half(a)
+        full, half = self.full[a], self.share(a)
         y, xh, c, up, dn, op = self.y, self.xh, self.c, self.up, self.dn, self.op
         if step == 0:
             self.local[a].wait()
-            self.send(a, 0, full.at[y, xh, c], full.at[y, xh, c], 0)
+            piece = full.at[y, xh, c, self.half(a, 1 - self.xl)]
+            self.send(a, 0, piece, piece, 0)
             piece = full.at[y, xh, c, half]
             self.send(a, 1, piece, piece, 1)
             self.send(a, 2, piece, piece, 2)
+        elif step == 10:
+            self.got(a, 0)
+            piece = full.at[y, 1 - xh, c, self.half(a, self.xl)]
+            self.send(a, 17, piece, piece, 6)
         elif step == 1:
-            self.got(a, 0)
+            self.got(a, 17)
             other = full.at[y, 1 - xh, c, half]
             self.send(a, 3, other, other, 1)
             self.send(a, 4, other, other, 2)
@@ -248,6 +259,15 @@
             for i, far in (((0, dn), (1, up)), ((2, op),))[step - 4]:
                 self.got(a, 7 + 2 * i)
                 self.got(a, 8 + 2 * i)
+                if a in QUARTERED:
+                    piece = full.at[far, :, c, self.half(a, self.xl)]
+                    self.send(a, 18 + i, piece, piece, 6)
+                else:
+                    piece = full.at[far, :, c]
+                    self.send(a, 14 + i, piece, piece, 5)
+        elif step in (11, 12):
+            for i, far in (((0, dn), (1, up)), ((2, op),))[step - 11]:
+                self.got(a, 18 + i)
                 piece = full.at[far, :, c]
                 self.send(a, 14 + i, piece, piece, 5)
         else:
@@ -260,19 +280,19 @@
 
 M, T, O, U, D = range(5)
 POINTS = {
-    "start": [(0, M), (0, O), (0, T), (0, U)],
-    "rolled": [(1, M), (1, O)],
-    "attention": [(2, M)],
-    "down": [(0, D), (1, T), (2, O), (4, M), (3, M)],
-    "merge": [(4, O), (2, T), (5, M), (3, O), (6, M), (7, M), (8, M), (9, M)],
-    "coarse": [(1, U), (3, T), (6, T)],
-    "coarse 1": [(4, T), (7, T), (8, T)],
-    "coarse 2": [(5, O), (2, U), (1, D), (5, T)],
-    "coarse 3": [(9, T)],
-    "coarse out": [(3, U), (6, O), (7, O), (8, O), (9, O)],
-    "hidden": [(4, U), (2, D), (6, U), (6, D)],
-    "hidden 1": [(5, U), (3, D), (4, D), (7, U), (7, D)],
-    "hidden 2": [(5, D), (8, U), (8, D)],
+    "start": [(0, M), (0, T), (0, O)],
+    "rolled": [(10, M), (1, M), (10, T), (0, U)],
+    "attention": [(2, M), (1, T), (10, O), (0, D)],
+    "down": [(3, M), (2, T), (1, O), (10, U), (4, M), (3, T), (2, O), (1, U)],
+    "merge": [(10, D), (5, M), (4, T), (3, O), (2, U), (1, D), (6, M), (7, M), (8, M), (9, M)],
+    "coarse": [(5, T), (4, O), (11, T), (6, T)],
+    "coarse 1": [(3, U), (2, D), (5, O), (12, T), (7, T), (8, T)],
+    "coarse 2": [(11, O), (4, U)],
+    "coarse 3": [(3, D), (12, O), (9, T)],
+    "coarse out": [(5, U), (6, O), (7, O), (8, O), (9, O)],
+    "hidden": [(4, D), (6, U), (6, D)],
+    "hidden 1": [(5, D), (7, U), (7, D)],
+    "hidden 2": [(8, U), (8, D)],
     "hidden 3": [(9, U), (9, D)],
 }
 
@@ -287,7 +307,8 @@
         f_merge, f_triple, f_output, f_up, f_down,
         x_ref, n_ref, lab_ref, qkv_ref, p_ref, mix_ref, res_ref, act_ref, slope_ref, win_ref,
         grad_ref, dres_ref, dqkv_ref,
-        j_ref, nj_ref, mg_ref, cn_ref, cqkv_ref, cp_ref, cmix_ref, cres_ref, cot_ref, hid_ref, dn_ref, cdqkv_ref,
+        j_ref, nj_ref, mg_ref, cn_ref, cqkv_ref, cp_ref, cmix_ref, cres_ref, cot_ref, hid_ref, dn_ref,
+        pt_ref, cpt_ref,
         halo_send, halo_recv, local_sem, send_sem, recv_sem, halo_ssem, halo_rsem,
     ) = refs
     gather = Gather(
@@ -362,8 +383,7 @@
                 q, k, v = (
                     qkv_ref[rows, h * 192 + 64 * i : h * 192 + 64 * i + 64].astype(BF16) for i in range(3)
                 )
-                p, m = attend(q, k, v, mask)
-                p_ref[w * 8 + h] = p
+                p_ref[w * 8 + h], pt_ref[w * 8 + h], m = attend(q, k, v, mask)
                 mixed.append(m)
             mix_ref[rows, pair * 128 : pair * 128 + 128] = jnp.concatenate(mixed, axis=-1)
 
@@ -439,8 +459,9 @@
         cqkv_ref[y] = packed
         for i in range(4):
             part = packed[:, i * 192 : i * 192 + 192].astype(BF16)
-            p, m = attend(part[:, :64], part[:, 64:128], part[:, 128:], None)
+            p, turned, m = attend(part[:, :64], part[:, 64:128], part[:, 128:], None)
             cp_ref[y * 4 + i] = p
+            cpt_ref[y * 4 + i] = turned
             mixed.append(m)
         cmix_ref[:, chunk(y, 256)] = jnp.concatenate(mixed, axis=-1).astype(BF16)
 
@@ -495,7 +516,8 @@
             part = cqkv_ref[y, :, i * 192 : i * 192 + 192].astype(BF16)
             packed.extend(
                 attend_pull(
-                    part[:, :64], part[:, 64:128], part[:, 128:], cp_ref[y * 4 + i], dmix[:, i * 64 : i * 64 + 64]
+                    part[:, :64], part[:, 64:128], part[:, 128:], cp_ref[y * 4 + i], cpt_ref[y * 4 + i],
+                    dmix[:, i * 64 : i * 64 + 64],
                 )
             )
         packed = jnp.concatenate(packed, axis=-1).astype(BF16)
@@ -567,7 +589,7 @@
                     qkv_ref[rows, h * 192 + 64 * i : h * 192 + 64 * i + 64].astype(BF16) for i in range(3)
                 )
                 dm = mix_ref[rows, h * 64 : h * 64 + 64].astype(BF16)
-                packed.extend(attend_pull(q, k, v, p_ref[w * 8 + h], dm))
+                packed.extend(attend_pull(q, k, v, p_ref[w * 8 + h], pt_ref[w * 8 + h], dm))
             dqkv_ref[rows, pair * 384 : pair * 384 + 384] = jnp.concatenate(packed, axis=-1)
 
     loop(4, fine_attention_pull)
@@ -619,7 +641,8 @@
         f32(288, 512), bf16(288, 2048), bf16(288, 2048), bf16(288, 512),
         f32(288, 512), f32(288, 512), f32(288, 1536),
         f32(288, 512), bf16(72, 2048), f32(72, 1024), bf16(72, 1024), f32(4, 72, 768), f32(16, 72, 72),
-        bf16(72, 1024), f32(72, 1024), f32(72, 1024), f32(72, 1024), f32(72, 1024), f32(8, 128),
+        bf16(72, 1024), f32(72, 1024), f32(72, 1024), f32(72, 1024), f32(72, 1024),
+        f32(32, 72, 72), f32(16, 72, 72),
         bf16(4, HALO, 512), bf16(4, HALO, 512),
         pltpu.SemaphoreType.DMA((5,)), pltpu.SemaphoreType.DMA((5, SLOTS)), pltpu.SemaphoreType.DMA((5, SLOTS)),
         pltpu.SemaphoreType.DMA((4, 3)), pltpu.SemaphoreType.DMA((4, 3)),

time: 150 us -> 145 us (0.967)
  Pallas kernels: 147 us -> 143 us
    pallas_call x1, Pallas kernels: 145 us -> 141 us  [local(): pl.pallas_call(kernel, out_shape=[jax.ShapeDtypeStruct((TOKENS, 512), BF1...]
where the time goes in v3:
time: 145 us
  Pallas kernels  143 us (99%)
    pallas_call x1, Pallas kernels, local(): pl.pallas_call(kernel, out_shape=[jax.ShapeDtypeStruct((TOKENS, 512), BF1...  141 us

profile of v3, /device:TPU:8, one launch (start us, length us, event | category | flops | bytes accessed | tf_op | source)
XLA Modules:
  0.0 145.3 jit_solution(16037663053146757411)
XLA Ops:
  0.6 1.3 reshape.22.refs_1_
  2.0 141.2 %backbone.1 = (bf16[288,512]{1,0:T(8,128)(2,1)}, bf16[6,12,1024]{2,1,0:T(8,128)(2,1)}, bf16[288,512]{1,0:T(8,128)(2,1)}) custom-call(bf16[288,512]{1,0:T(8,128)(2,1)} %bitcast.11, s32[1,288]{1,0:T(1,128)} %reshape.22.refs_1_, f32[1,512]{1,0:T(1,128)} %bitcast.16, bf16[512,1536]{1,0:T(8,128)(2,1)} %refs_3_.1, bf16[512,512]{1,0:T(8,128)(2,1)} %refs_4_.1, ...), custom_call_target="tpu_custom_call" | custom-call | tf_op jit(solution)/shard_map/backbone/pallas_call | solution.py:650
  143.2 2.0 %results.1 = (bf16[288,512]{1,0:T(8,128)(2,1)}, bf16[6,12,1024]{2,1,0:T(8,128)(2,1)}, bf16[288,512]{1,0:T(8,128)(2,1)}) custom-call(bf16[288,512]{1,0:T(8,128)(2,1)} %get-tuple-element.9.refs_0_, bf16[6,12,1024]{2,1,0:T(8,128)(2,1)} %get-tuple-element.10.refs_1_, bf16[288,512]{1,0:T(8,128)(2,1)} %get-tuple-element.11.refs_2_), custom_call_target="tpu_custom_call" | custom-call | tf_op jit(solution)/shard_map/results/pallas_call | solution.py:665

commit v4 on v3

--- a/solution.py
+++ b/solution.py
@@ -308,7 +308,7 @@
         x_ref, n_ref, lab_ref, qkv_ref, p_ref, mix_ref, res_ref, act_ref, slope_ref, win_ref,
         grad_ref, dres_ref, dqkv_ref,
         j_ref, nj_ref, mg_ref, cn_ref, cqkv_ref, cp_ref, cmix_ref, cres_ref, cot_ref, hid_ref, dn_ref,
-        pt_ref, cpt_ref,
+        pt_ref, cpt_ref, lifted_ref,
         halo_send, halo_recv, local_sem, send_sem, recv_sem, halo_ssem, halo_rsem,
     ) = refs
     gather = Gather(
@@ -492,13 +492,11 @@
             active.append(value.astype(BF16))
             total = total + mm_t((grad[:, i * 256 : i * 256 + 256] * slope).astype(BF16), upper)
         dn_ref[...] = total
-        hid_ref[...] += mm(jnp.concatenate(active, axis=-1), lower_weight)
+        lifted_ref[y] = jnp.concatenate(active, axis=-1)
 
     for name, y in zip(("hidden", "hidden 1", "hidden 2", "hidden 3"), order):
         point(name)
         coarse_hidden(y)
-    for i in range(6):
-        coarse_out[i] = hid_ref[i * 12 : i * 12 + 12].astype(BF16)
     xhat, scale = standard(cres_ref[...])
     cres_ref[...] = cot_ref[...] + norm_pull(dn_ref[...], cg2[...], xhat, scale)
 
@@ -549,6 +547,13 @@
     win_ref[...] = grad_ref[...].astype(BF16)
     copies = exchange(2, mm(m_join_pack[...], win_ref[...]), ahead)
     grad_ref[...] = mm(m_join_own[...], win_ref[...])
+
+    def coarse_lower(y):
+        hid_ref[...] += mm(lifted_ref[y], f_down[y].reshape(1024, 1024))
+
+    loop(4, coarse_lower)
+    for i in range(6):
+        coarse_out[i] = hid_ref[i * 12 : i * 12 + 12].astype(BF16)
     settle(copies)
     grad_ref[...] += mm(m_roll_got[...], halo_recv[2])
 
@@ -642,7 +647,7 @@
         f32(288, 512), f32(288, 512), f32(288, 1536),
         f32(288, 512), bf16(72, 2048), f32(72, 1024), bf16(72, 1024), f32(4, 72, 768), f32(16, 72, 72),
         bf16(72, 1024), f32(72, 1024), f32(72, 1024), f32(72, 1024), f32(72, 1024),
-        f32(32, 72, 72), f32(16, 72, 72),
+        f32(32, 72, 72), f32(16, 72, 72), bf16(4, 72, 1024),
         bf16(4, HALO, 512), bf16(4, HALO, 512),
         pltpu.SemaphoreType.DMA((5,)), pltpu.SemaphoreType.DMA((5, SLOTS)), pltpu.SemaphoreType.DMA((5, SLOTS)),
         pltpu.SemaphoreType.DMA((4, 3)), pltpu.SemaphoreType.DMA((4, 3)),

time: 145 us -> 145 us (level)
  no operation moved by 1% of the time
where the time goes in v4:
time: 145 us
  Pallas kernels  143 us (99%)
    pallas_call x1, Pallas kernels, local(): pl.pallas_call(kernel, out_shape=[jax.ShapeDtypeStruct((TOKENS, 512), BF1...  140 us

profile of v4, /device:TPU:8, one launch (start us, length us, event | category | flops | bytes accessed | tf_op | source)
XLA Modules:
  0.0 144.5 jit_solution(11578441298108283831)
XLA Ops:
  0.6 1.3 reshape.22.refs_1_
  2.0 140.5 %backbone.1 = (bf16[288,512]{1,0:T(8,128)(2,1)}, bf16[6,12,1024]{2,1,0:T(8,128)(2,1)}, bf16[288,512]{1,0:T(8,128)(2,1)}) custom-call(bf16[288,512]{1,0:T(8,128)(2,1)} %bitcast.11, s32[1,288]{1,0:T(1,128)} %reshape.22.refs_1_, f32[1,512]{1,0:T(1,128)} %bitcast.16, bf16[512,1536]{1,0:T(8,128)(2,1)} %refs_3_.1, bf16[512,512]{1,0:T(8,128)(2,1)} %refs_4_.1, ...), custom_call_target="tpu_custom_call" | custom-call | tf_op jit(solution)/shard_map/backbone/pallas_call | solution.py:655
  142.5 2.0 %results.1 = (bf16[288,512]{1,0:T(8,128)(2,1)}, bf16[6,12,1024]{2,1,0:T(8,128)(2,1)}, bf16[288,512]{1,0:T(8,128)(2,1)}) custom-call(bf16[288,512]{1,0:T(8,128)(2,1)} %get-tuple-element.9.refs_0_, bf16[6,12,1024]{2,1,0:T(8,128)(2,1)} %get-tuple-element.10.refs_1_, bf16[288,512]{1,0:T(8,128)(2,1)} %get-tuple-element.11.refs_2_), custom_call_target="tpu_custom_call" | custom-call | tf_op jit(solution)/shard_map/results/pallas_call | solution.py:670
